TPU v7x, 512 devices: a whole 4x8x8 slice. The times are simulated.
512 devices in a mesh: outer: 16 (over y_hi, z), inner: 32 (over y_lo, x, core).
Axes of the slice: x: 4, y: 8 (y_hi: 2, y_lo: 4; y = y_hi * 4 + y_lo), z: 8, core: 2. Of those that a mesh axis runs over, the one named last changes fastest.
Arguments:
- queries: bfloat16 [65536, 32, 128], P(('outer', 'inner')), may hold values from -8 to 8
- key_states: bfloat16 [65536, 4, 128], P(('outer', 'inner')), may hold values from -8 to 8
- value_states: bfloat16 [65536, 4, 128], P(('outer', 'inner')), may hold values from -6 to 6
- out_grad: bfloat16 [65536, 32, 128], P(('outer', 'inner')), may hold values from -6 to 6
- bounds: int32 [3, 65536], P(None, ('outer', 'inner')), may hold values from 0 to 65535, as said below
Outputs:
- query_grad: bfloat16 [65536, 32, 128], P(('outer', 'inner'))
- key_grad: bfloat16 [65536, 4, 128], P(('outer', 'inner'))
- value_grad: bfloat16 [65536, 4, 128], P(('outer', 'inner'))
Inputs may be any that keep to these rules, and one draw needn't show every extreme that they name: For each token t, bounds[0, t] is the first token of t's document (tokens of a document are consecutive), with t - 512 < bounds[0, t] <= t; in every draw some token has t - bounds[0, t] = 511. Either bounds[1, t] = bounds[2, t] = 0, or bounds[0, t] + 2 <= bounds[1, t] < bounds[2, t] <= t.
All inputs are finite; a program needn't handle non-finite values.
Results may differ from a plain program's by a relative error of at most 0.006.
Values may be sent and summed in bfloat16 or wider, within the bound.
A program may use at most 64 MiB of HBM per device.

v0:
```python
import jax
import jax.numpy as jnp
from jax import lax
from jax.sharding import PartitionSpec as P

QH = 32
KVH = 4
HD = 128
SPAN = 4


def from_behind(shard, axis, by):
    peers = lax.axis_size(axis)
    pairs = [(i, i + by) for i in range(peers) if 0 <= i + by < peers]
    return lax.ppermute(shard, axis, pairs)


def shifted(shard, axis, by):
    peers = lax.axis_size(axis)
    return lax.ppermute(shard, axis, [(i, (i + by) % peers) for i in range(peers)])


def visible(query_pos, key_pos, bounds):
    doc_start = bounds[0][:, None]
    skip_low = bounds[1][:, None]
    skip_high = bounds[2][:, None]
    key_row = key_pos[None, :]
    return (
        (key_row >= doc_start)
        & (key_row <= query_pos[:, None])
        & ((key_row < skip_low) | (key_row >= skip_high))
    )


def per_device(queries, key_states, value_states, out_grad, bounds):
    token_rows = queries.shape[0]
    group_size = QH // KVH
    score_scale = HD ** (-0.5)
    my_index = lax.axis_index(("outer", "inner"))
    query_pos = my_index * token_rows + jnp.arange(token_rows, dtype=jnp.int32)
    query_four = queries.reshape(token_rows, KVH, group_size, HD)
    grad_four = out_grad.reshape(token_rows, KVH, group_size, HD)

    def seen_at(offset):
        key_pos = (my_index - offset) * token_rows + jnp.arange(token_rows, dtype=jnp.int32)
        return visible(query_pos, key_pos, bounds)

    def guarded(offset, compute):
        if offset == 0:
            return compute()
        return compute()

    def project(key_block, value_block):
        scores = (
            jnp.einsum("tkgd,skd->kgts", query_four, key_block, preferred_element_type=jnp.float32)
            * score_scale
        )
        grad_weights = jnp.einsum(
            "tkgd,skd->kgts", grad_four, value_block, preferred_element_type=jnp.float32
        )
        return (scores, grad_weights)

    def absorb(running, key_block, value_block, offset):
        row_max, row_total, weighted = running
        seen_mask = seen_at(offset)
        scores, grad_weights = project(key_block, value_block)
        new_max = jnp.maximum(row_max, jnp.max(jnp.where(seen_mask, scores, -jnp.inf), axis=-1))
        rescale = jnp.exp(row_max - new_max)
        weights = jnp.exp(jnp.where(seen_mask, scores - new_max[..., None], -jnp.inf))
        return (
            new_max,
            row_total * rescale + jnp.sum(weights, axis=-1),
            weighted * rescale + jnp.sum(weights * grad_weights, axis=-1),
        )

    stat_shape = (KVH, group_size, token_rows)
    running = (
        jnp.full(stat_shape, -jnp.inf, jnp.float32),
        jnp.zeros(stat_shape, jnp.float32),
        jnp.zeros(stat_shape, jnp.float32),
    )
    running = absorb(running, key_states, value_states, 0)
    kept = [(key_states, value_states)]
    key_now, value_now = (key_states, value_states)
    for offset in range(1, SPAN + 1):
        key_now, value_now = from_behind((key_now, value_now), ("outer", "inner"), 1)
        kept.append((key_now, value_now))
        previous = running
        running = guarded(offset, lambda: absorb(previous, key_now, value_now, offset))
    row_max, row_total, weighted = running
    log_total = row_max + jnp.log(row_total)
    row_delta = weighted / row_total

    def partial_value(key_block, value_block, offset):
        seen_mask = seen_at(offset)
        scores, grad_weights = project(key_block, value_block)
        prob = jnp.exp(jnp.where(seen_mask, scores - log_total[..., None], -jnp.inf))
        weights = prob.astype(jnp.bfloat16)
        dscore = (score_scale * prob * (grad_weights - row_delta[..., None])).astype(jnp.bfloat16)
        query_part = jnp.einsum(
            "kgts,skd->tkgd", dscore, key_block, preferred_element_type=jnp.float32
        )
        key_part = jnp.einsum(
            "kgts,tkgd->skd", dscore, query_four, preferred_element_type=jnp.float32
        )
        value_part = jnp.einsum(
            "kgts,tkgd->skd", weights, grad_four, preferred_element_type=jnp.float32
        )
        return (query_part, key_part, value_part)

    query_sum = jnp.zeros((token_rows, KVH, group_size, HD), jnp.float32)
    carried = (
        jnp.zeros((token_rows, KVH, HD), jnp.float32),
        jnp.zeros((token_rows, KVH, HD), jnp.float32),
    )
    owned = (
        jnp.zeros((token_rows, KVH, HD), jnp.float32),
        jnp.zeros((token_rows, KVH, HD), jnp.float32),
    )
    for offset in range(SPAN + 1):
        key_now, value_now = kept[offset]
        if offset > 0:
            carried = shifted((carried[0], carried[1]), ("outer", "inner"), 1)
        query_part, key_part, value_part = guarded(
            offset, lambda: partial_value(key_now, value_now, offset)
        )
        query_sum = query_sum + query_part
        carried = (carried[0] + key_part, carried[1] + value_part)
    owned = (
        shifted(carried[0].astype(jnp.bfloat16), ("outer", "inner"), -SPAN).astype(jnp.float32),
        shifted(carried[1].astype(jnp.bfloat16), ("outer", "inner"), -SPAN).astype(jnp.float32),
    )
    query_grad = query_sum.reshape(token_rows, QH, HD).astype(jnp.bfloat16)
    return (query_grad, owned[0].astype(jnp.bfloat16), owned[1].astype(jnp.bfloat16))


def solution(mesh):
    in_specs = (
        P(("outer", "inner"), None, None),
        P(("outer", "inner"), None, None),
        P(("outer", "inner"), None, None),
        P(("outer", "inner"), None, None),
        P(None, ("outer", "inner")),
    )
    out_specs = (
        P(("outer", "inner"), None, None),
        P(("outer", "inner"), None, None),
        P(("outer", "inner"), None, None),
    )
    return jax.shard_map(
        per_device, mesh=mesh, in_specs=in_specs, out_specs=out_specs, check_vma=False
    )
```

profile of v0, /device:TPU:252, one launch (start us, length us, event | category | flops | bytes accessed | tf_op | source)
XLA Modules:
  0.0 141.4 jit_solution(10639727233248336888)
XLA Ops:
  1.7 1.9 %collective-permute-start.4 = (bf16[128,4,128]{2,0,1:T(8,128)(2,1)S(1)}, bf16[128,4,128]{2,0,1:T(8,128)(2,1)S(1)}, u32[]{:S(2)}, u32[]{:S(2)}) collective-permute-start(bf16[128,4,128]{2,0,1:T(8,128)(2,1)S(1)} %copy.17), channel_id=1, source_target_pairs={{0,1},{1,2},{2,3},{3,4},{4,5},{5,6},{6,7},{7,8},{8,9},{9,10},{10,1... | collective-permute-start | bytes 393224 | tf_op jit(solution)/shard_map/ppermute | solution.py:15
  4.5 3.2 %collective-permute-start = (bf16[128,4,128]{2,0,1:T(8,128)(2,1)S(1)}, bf16[128,4,128]{2,0,1:T(8,128)(2,1)S(1)}, u32[]{:S(2)}, u32[]{:S(2)}) collective-permute-start(bf16[128,4,128]{2,0,1:T(8,128)(2,1)S(1)} %copy.10), channel_id=1, source_target_pairs={{0,1},{1,2},{2,3},{3,4},{4,5},{5,6},{6,7},{7,8},{8,9},{9,10},{10,1... | collective-permute-start | bytes 393224 | tf_op jit(solution)/shard_map/ppermute | solution.py:15
  8.8 2.0 %fusion.35 = (f32[4,8,128]{2,1,0:T(8,128)S(1)}, f32[4,128,128,8]{2,1,3,0:T(8,128)S(1)}) fusion(pred[128,128]{0,1:T(8,128)(4,1)S(1)} %get-tuple-element.31, bf16[128,4,8,128]{3,2,1,0:T(8,128)(2,1)} %bitcast.312, bf16[128,4,128,1]{2,1,0,3:T(4,128)(2,1)} %bitcast.323), kind=kOutput, calls=%fused_computation.60 | convolution fusion | flops 135786496 | bytes 3309568 | tf_op jit(solution)/shard_map/tkgd,skd->kgts/dot_general | solution.py:55
  11.8 1.9 %collective-permute-start.5 = (bf16[128,4,128]{2,0,1:T(8,128)(2,1)S(1)}, bf16[128,4,128]{2,0,1:T(8,128)(2,1)S(1)}, u32[]{:S(2)}, u32[]{:S(2)}) collective-permute-start(bf16[128,4,128]{2,0,1:T(8,128)(2,1)S(1)} %collective-permute-done.4), channel_id=1, source_target_pairs={{0,1},{1,2},{2,3},{3,4},{4,5},{5,6},{6,7},{7,8},{8,9},{9,10},{10,1... | collective-permute-start | bytes 393224 | tf_op jit(solution)/shard_map/ppermute | solution.py:15
  13.7 7.9 %collective-permute-start.1 = (bf16[128,4,128]{2,0,1:T(8,128)(2,1)S(1)}, bf16[128,4,128]{2,0,1:T(8,128)(2,1)S(1)}, u32[]{:S(2)}, u32[]{:S(2)}) collective-permute-start(bf16[128,4,128]{2,0,1:T(8,128)(2,1)S(1)} %collective-permute-done), channel_id=1, source_target_pairs={{0,1},{1,2},{2,3},{3,4},{4,5},{5,6},{6,7},{7,8},{8,9},{9,10},{10,1... | collective-permute-start | bytes 393224 | tf_op jit(solution)/shard_map/ppermute | solution.py:15
  22.3 1.9 %collective-permute-start.6 = (bf16[128,4,128]{2,0,1:T(8,128)(2,1)S(1)}, bf16[128,4,128]{2,0,1:T(8,128)(2,1)S(1)}, u32[]{:S(2)}, u32[]{:S(2)}) collective-permute-start(bf16[128,4,128]{2,0,1:T(8,128)(2,1)S(1)} %collective-permute-done.5), channel_id=1, source_target_pairs={{0,1},{1,2},{2,3},{3,4},{4,5},{5,6},{6,7},{7,8},{8,9},{9,10},{10,1... | collective-permute-start | bytes 393224 | tf_op jit(solution)/shard_map/ppermute | solution.py:15
  24.3 5.4 %collective-permute-start.2 = (bf16[128,4,128]{2,0,1:T(8,128)(2,1)S(1)}, bf16[128,4,128]{2,0,1:T(8,128)(2,1)S(1)}, u32[]{:S(2)}, u32[]{:S(2)}) collective-permute-start(bf16[128,4,128]{2,0,1:T(8,128)(2,1)S(1)} %collective-permute-done.1), channel_id=1, source_target_pairs={{0,1},{1,2},{2,3},{3,4},{4,5},{5,6},{6,7},{7,8},{8,9},{9,10},{10,1... | collective-permute-start | bytes 393224 | tf_op jit(solution)/shard_map/ppermute | solution.py:15
  30.3 2.8 %collective-permute-start.7 = (bf16[128,4,128]{2,0,1:T(8,128)(2,1)S(1)}, bf16[128,4,128]{2,0,1:T(8,128)(2,1)S(1)}, u32[]{:S(2)}, u32[]{:S(2)}) collective-permute-start(bf16[128,4,128]{2,0,1:T(8,128)(2,1)S(1)} %collective-permute-done.6), channel_id=1, source_target_pairs={{0,1},{1,2},{2,3},{3,4},{4,5},{5,6},{6,7},{7,8},{8,9},{9,10},{10,1... | collective-permute-start | bytes 393224 | tf_op jit(solution)/shard_map/ppermute | solution.py:15
  33.2 8.9 %collective-permute-start.3 = (bf16[128,4,128]{2,0,1:T(8,128)(2,1)S(1)}, bf16[128,4,128]{2,0,1:T(8,128)(2,1)S(1)}, u32[]{:S(2)}, u32[]{:S(2)}) collective-permute-start(bf16[128,4,128]{2,0,1:T(8,128)(2,1)S(1)} %collective-permute-done.2), channel_id=1, source_target_pairs={{0,1},{1,2},{2,3},{3,4},{4,5},{5,6},{6,7},{7,8},{8,9},{9,10},{10,1... | collective-permute-start | bytes 393224 | tf_op jit(solution)/shard_map/ppermute | solution.py:15
  47.7 1.6 %convolution_bitcast_fusion.4 = f32[128,4,128]{2,0,1:T(8,128)} fusion(f32[4,128,128,8]{2,1,3,0:T(8,128)S(1)} %get-tuple-element.42, f32[4,8,128]{2,1,0:T(8,128)S(1)} %get-tuple-element.20, pred[128,128]{0,1:T(8,128)(4,1)S(1)} %get-tuple-element.31, bf16[128,4,8,128]{3,2,1,0:T(8,128)(2,1)S(1)} %bitcast.307), kind=kOutput, calls=%fused_computation.80 | convolution fusion | flops 136314880 | bytes 3440640 | tf_op jit(solution)/shard_map/kgts,tkgd->skd/dot_general | solution.py:106
  54.0 3.3 %fusion.2 = (bf16[4,8,128,128]{2,3,1,0:T(8,128)(2,1)S(1)}, bf16[4,8,128,128]{2,3,1,0:T(8,128)(2,1)S(1)}, bf16[4,8,128,128]{2,3,1,0:T(8,128)(2,1)S(1)}, bf16[4,8,...) fusion(f32[4,128,128,8]{2,1,3,0:T(8,128)S(1)} %get-tuple-element.45, f32[4,128,128,8]{2,1,3,0:T(8,128)S(1)} %get-tuple-element.36, ...), kind=kLoop, calls=%fused_computation.4 | loop fusion | flops 18350080 | bytes 26329088 | tf_op jit(solution)/shard_map/convert_element_type | solution.py:99
  58.8 3.8 %collective-permute-start.8 = (f32[128,4,128]{2,0,1:T(8,128)S(1)}, f32[128,4,128]{2,0,1:T(8,128)S(1)}, u32[]{:S(2)}, u32[]{:S(2)}) collective-permute-start(f32[128,4,128]{2,0,1:T(8,128)S(1)} %convolution_bitcast_fusion.9), channel_id=1, source_target_pairs={{0,1},{1,2},{2,3},{3,4},{4,5},{5,6},{6,7},{7,8},{8,9},{9,10},{10,1... | collective-permute-start | bytes 786440 | tf_op jit(solution)/shard_map/ppermute | solution.py:20
  62.6 8.0 %collective-permute-start.13 = (f32[128,4,128]{2,0,1:T(8,128)S(1)}, f32[128,4,128]{2,0,1:T(8,128)S(1)}, u32[]{:S(2)}, u32[]{:S(2)}) collective-permute-start(f32[128,4,128]{2,0,1:T(8,128)S(1)} %copy-done.9), channel_id=1, source_target_pairs={{0,1},{1,2},{2,3},{3,4},{4,5},{5,6},{6,7},{7,8},{8,9},{9,10},{10,1... | collective-permute-start | bytes 786440 | tf_op jit(solution)/shard_map/ppermute | solution.py:20
  72.4 3.8 %collective-permute-start.9 = (f32[128,4,128]{2,0,1:T(8,128)S(1)}, f32[128,4,128]{2,0,1:T(8,128)S(1)}, u32[]{:S(2)}, u32[]{:S(2)}) collective-permute-start(f32[128,4,128]{2,0,1:T(8,128)S(1)} %fusion.50), channel_id=1, source_target_pairs={{0,1},{1,2},{2,3},{3,4},{4,5},{5,6},{6,7},{7,8},{8,9},{9,10},{10,1... | collective-permute-start | bytes 786440 | tf_op jit(solution)/shard_map/ppermute | solution.py:20
  77.1 10.4 %collective-permute-start.14 = (f32[128,4,128]{2,0,1:T(8,128)S(1)}, f32[128,4,128]{2,0,1:T(8,128)S(1)}, u32[]{:S(2)}, u32[]{:S(2)}) collective-permute-start(f32[128,4,128]{2,0,1:T(8,128)S(1)} %fusion.51), channel_id=1, source_target_pairs={{0,1},{1,2},{2,3},{3,4},{4,5},{5,6},{6,7},{7,8},{8,9},{9,10},{10,1... | collective-permute-start | bytes 786440 | tf_op jit(solution)/shard_map/ppermute | solution.py:20
  87.5 2.4 %collective-permute-start.10 = (f32[128,4,128]{2,0,1:T(8,128)S(1)}, f32[128,4,128]{2,0,1:T(8,128)S(1)}, u32[]{:S(2)}, u32[]{:S(2)}) collective-permute-start(f32[128,4,128]{2,0,1:T(8,128)S(1)} %add.235), channel_id=1, source_target_pairs={{0,1},{1,2},{2,3},{3,4},{4,5},{5,6},{6,7},{7,8},{8,9},{9,10},{10,1... | collective-permute-start | bytes 786440 | tf_op jit(solution)/shard_map/ppermute | solution.py:20
  91.1 10.1 %collective-permute-start.15 = (f32[128,4,128]{2,0,1:T(8,128)S(1)}, f32[128,4,128]{2,0,1:T(8,128)S(1)}, u32[]{:S(2)}, u32[]{:S(2)}) collective-permute-start(f32[128,4,128]{2,0,1:T(8,128)S(1)} %add.239), channel_id=1, source_target_pairs={{0,1},{1,2},{2,3},{3,4},{4,5},{5,6},{6,7},{7,8},{8,9},{9,10},{10,1... | collective-permute-start | bytes 786440 | tf_op jit(solution)/shard_map/ppermute | solution.py:20
  101.3 2.4 %collective-permute-start.11 = (f32[128,4,128]{2,0,1:T(8,128)S(1)}, f32[128,4,128]{2,0,1:T(8,128)S(1)}, u32[]{:S(2)}, u32[]{:S(2)}) collective-permute-start(f32[128,4,128]{2,0,1:T(8,128)S(1)} %add.236), channel_id=1, source_target_pairs={{0,1},{1,2},{2,3},{3,4},{4,5},{5,6},{6,7},{7,8},{8,9},{9,10},{10,1... | collective-permute-start | bytes 786440 | tf_op jit(solution)/shard_map/ppermute | solution.py:20
  104.2 10.5 %collective-permute-start.16 = (f32[128,4,128]{2,0,1:T(8,128)S(1)}, f32[128,4,128]{2,0,1:T(8,128)S(1)}, u32[]{:S(2)}, u32[]{:S(2)}) collective-permute-start(f32[128,4,128]{2,0,1:T(8,128)S(1)} %add.240), channel_id=1, source_target_pairs={{0,1},{1,2},{2,3},{3,4},{4,5},{5,6},{6,7},{7,8},{8,9},{9,10},{10,1... | collective-permute-start | bytes 786440 | tf_op jit(solution)/shard_map/ppermute | solution.py:20
  115.4 1.9 %collective-permute-start.12 = (bf16[128,4,128]{2,0,1:T(8,128)(2,1)S(1)}, bf16[128,4,128]{2,0,1:T(8,128)(2,1)S(1)}, u32[]{:S(2)}, u32[]{:S(2)}) collective-permute-start(bf16[128,4,128]{2,0,1:T(8,128)(2,1)S(1)} %add_convert_fusion.2), channel_id=1, source_target_pairs={{0,508},{1,509},{2,510},{3,511},{4,0},{5,1},{6,2},{7,3},{8,4},{9,5... | collective-permute-start | bytes 393224 | tf_op jit(solution)/shard_map/ppermute | solution.py:20
  117.4 1.9 %collective-permute-start.17 = (bf16[128,4,128]{2,0,1:T(8,128)(2,1)S(1)}, bf16[128,4,128]{2,0,1:T(8,128)(2,1)S(1)}, u32[]{:S(2)}, u32[]{:S(2)}) collective-permute-start(bf16[128,4,128]{2,0,1:T(8,128)(2,1)S(1)} %add_convert_fusion.1), channel_id=1, source_target_pairs={{0,508},{1,509},{2,510},{3,511},{4,0},{5,1},{6,2},{7,3},{8,4},{9,5... | collective-permute-start | bytes 393224 | tf_op jit(solution)/shard_map/ppermute | solution.py:20
  120.2 1.6 %copy.38 = bf16[128,32,128]{2,1,0:T(8,128)(2,1)} copy(bf16[128,32,128]{2,0,1:T(8,128)(2,1)S(1)} %bitcast.322) | data formatting | bytes 2097152
  121.9 14.0 %collective-permute-done.12 = bf16[128,4,128]{2,0,1:T(8,128)(2,1)S(1)} collective-permute-done((bf16[128,4,128]{2,0,1:T(8,128)(2,1)S(1)}, bf16[128,4,128]{2,0,1:T(8,128)(2,1)S(1)}, u32[]{:S(2)}, u32[]{:S(2)}) %collective-permute-start.12) | collective-permute-done | bytes 131104 | tf_op jit(solution)/shard_map/ppermute | solution.py:20
  136.7 3.9 %collective-permute-done.17 = bf16[128,4,128]{2,0,1:T(8,128)(2,1)S(1)} collective-permute-done((bf16[128,4,128]{2,0,1:T(8,128)(2,1)S(1)}, bf16[128,4,128]{2,0,1:T(8,128)(2,1)S(1)}, u32[]{:S(2)}, u32[]{:S(2)}) %collective-permute-start.17) | collective-permute-done | bytes 131104 | tf_op jit(solution)/shard_map/ppermute | solution.py:20
  (76 shorter events, 24.5 us)
Async XLA Ops:
  0.6 10.1 %copy-start = (bf16[128,32,128]{2,1,0:T(8,128)(2,1)S(1)}, bf16[128,32,128]{2,1,0:T(8,128)(2,1)}, u32[]{:S(2)}) copy-start(bf16[128,32,128]{2,1,0:T(8,128)(2,1)} %param.8) | copy-start | bytes 3145732
  0.6 10.1 %copy-start.3 = (bf16[128,4,128]{2,1,0:T(4,128)(2,1)S(1)}, bf16[128,4,128]{2,1,0:T(4,128)(2,1)}, u32[]{:S(2)}) copy-start(bf16[128,4,128]{2,1,0:T(4,128)(2,1)} %param.7) | copy-start | bytes 393220
  1.7 10.1 %collective-permute-start.4 = (bf16[128,4,128]{2,0,1:T(8,128)(2,1)S(1)}, bf16[128,4,128]{2,0,1:T(8,128)(2,1)S(1)}, u32[]{:S(2)}, u32[]{:S(2)}) collective-permute-start(bf16[128,4,128]{2,0,1:T(8,128)(2,1)S(1)} %copy.17), channel_id=1, source_target_pairs={{0,1},{1,2},{2,3},{3,4},{4,5},{5,6},{6,7},{7,8},{8,9},{9,10},{10,1... | collective-permute-start | bytes 393224 | tf_op jit(solution)/shard_map/ppermute | solution.py:15
  4.5 9.2 %collective-permute-start = (bf16[128,4,128]{2,0,1:T(8,128)(2,1)S(1)}, bf16[128,4,128]{2,0,1:T(8,128)(2,1)S(1)}, u32[]{:S(2)}, u32[]{:S(2)}) collective-permute-start(bf16[128,4,128]{2,0,1:T(8,128)(2,1)S(1)} %copy.10), channel_id=1, source_target_pairs={{0,1},{1,2},{2,3},{3,4},{4,5},{5,6},{6,7},{7,8},{8,9},{9,10},{10,1... | collective-permute-start | bytes 393224 | tf_op jit(solution)/shard_map/ppermute | solution.py:15
  10.8 10.8 %copy-start.1 = (bf16[128,32,128]{2,1,0:T(8,128)(2,1)S(1)}, bf16[128,32,128]{2,1,0:T(8,128)(2,1)}, u32[]{:S(2)}) copy-start(bf16[128,32,128]{2,1,0:T(8,128)(2,1)} %param.5) | copy-start | bytes 3145732
  11.8 10.5 %collective-permute-start.5 = (bf16[128,4,128]{2,0,1:T(8,128)(2,1)S(1)}, bf16[128,4,128]{2,0,1:T(8,128)(2,1)S(1)}, u32[]{:S(2)}, u32[]{:S(2)}) collective-permute-start(bf16[128,4,128]{2,0,1:T(8,128)(2,1)S(1)} %collective-permute-done.4), channel_id=1, source_target_pairs={{0,1},{1,2},{2,3},{3,4},{4,5},{5,6},{6,7},{7,8},{8,9},{9,10},{10,1... | collective-permute-start | bytes 393224 | tf_op jit(solution)/shard_map/ppermute | solution.py:15
  13.7 10.5 %collective-permute-start.1 = (bf16[128,4,128]{2,0,1:T(8,128)(2,1)S(1)}, bf16[128,4,128]{2,0,1:T(8,128)(2,1)S(1)}, u32[]{:S(2)}, u32[]{:S(2)}) collective-permute-start(bf16[128,4,128]{2,0,1:T(8,128)(2,1)S(1)} %collective-permute-done), channel_id=1, source_target_pairs={{0,1},{1,2},{2,3},{3,4},{4,5},{5,6},{6,7},{7,8},{8,9},{9,10},{10,1... | collective-permute-start | bytes 393224 | tf_op jit(solution)/shard_map/ppermute | solution.py:15
  22.3 8.0 %collective-permute-start.6 = (bf16[128,4,128]{2,0,1:T(8,128)(2,1)S(1)}, bf16[128,4,128]{2,0,1:T(8,128)(2,1)S(1)}, u32[]{:S(2)}, u32[]{:S(2)}) collective-permute-start(bf16[128,4,128]{2,0,1:T(8,128)(2,1)S(1)} %collective-permute-done.5), channel_id=1, source_target_pairs={{0,1},{1,2},{2,3},{3,4},{4,5},{5,6},{6,7},{7,8},{8,9},{9,10},{10,1... | collective-permute-start | bytes 393224 | tf_op jit(solution)/shard_map/ppermute | solution.py:15
  24.3 8.9 %collective-permute-start.2 = (bf16[128,4,128]{2,0,1:T(8,128)(2,1)S(1)}, bf16[128,4,128]{2,0,1:T(8,128)(2,1)S(1)}, u32[]{:S(2)}, u32[]{:S(2)}) collective-permute-start(bf16[128,4,128]{2,0,1:T(8,128)(2,1)S(1)} %collective-permute-done.1), channel_id=1, source_target_pairs={{0,1},{1,2},{2,3},{3,4},{4,5},{5,6},{6,7},{7,8},{8,9},{9,10},{10,1... | collective-permute-start | bytes 393224 | tf_op jit(solution)/shard_map/ppermute | solution.py:15
  30.3 16.3 %collective-permute-start.7 = (bf16[128,4,128]{2,0,1:T(8,128)(2,1)S(1)}, bf16[128,4,128]{2,0,1:T(8,128)(2,1)S(1)}, u32[]{:S(2)}, u32[]{:S(2)}) collective-permute-start(bf16[128,4,128]{2,0,1:T(8,128)(2,1)S(1)} %collective-permute-done.6), channel_id=1, source_target_pairs={{0,1},{1,2},{2,3},{3,4},{4,5},{5,6},{6,7},{7,8},{8,9},{9,10},{10,1... | collective-permute-start | bytes 393224 | tf_op jit(solution)/shard_map/ppermute | solution.py:15
  33.2 9.7 %collective-permute-start.3 = (bf16[128,4,128]{2,0,1:T(8,128)(2,1)S(1)}, bf16[128,4,128]{2,0,1:T(8,128)(2,1)S(1)}, u32[]{:S(2)}, u32[]{:S(2)}) collective-permute-start(bf16[128,4,128]{2,0,1:T(8,128)(2,1)S(1)} %collective-permute-done.2), channel_id=1, source_target_pairs={{0,1},{1,2},{2,3},{3,4},{4,5},{5,6},{6,7},{7,8},{8,9},{9,10},{10,1... | collective-permute-start | bytes 393224 | tf_op jit(solution)/shard_map/ppermute | solution.py:15
  58.8 13.0 %collective-permute-start.8 = (f32[128,4,128]{2,0,1:T(8,128)S(1)}, f32[128,4,128]{2,0,1:T(8,128)S(1)}, u32[]{:S(2)}, u32[]{:S(2)}) collective-permute-start(f32[128,4,128]{2,0,1:T(8,128)S(1)} %convolution_bitcast_fusion.9), channel_id=1, source_target_pairs={{0,1},{1,2},{2,3},{3,4},{4,5},{5,6},{6,7},{7,8},{8,9},{9,10},{10,1... | collective-permute-start | bytes 786440 | tf_op jit(solution)/shard_map/ppermute | solution.py:20
  62.6 13.5 %collective-permute-start.13 = (f32[128,4,128]{2,0,1:T(8,128)S(1)}, f32[128,4,128]{2,0,1:T(8,128)S(1)}, u32[]{:S(2)}, u32[]{:S(2)}) collective-permute-start(f32[128,4,128]{2,0,1:T(8,128)S(1)} %copy-done.9), channel_id=1, source_target_pairs={{0,1},{1,2},{2,3},{3,4},{4,5},{5,6},{6,7},{7,8},{8,9},{9,10},{10,1... | collective-permute-start | bytes 786440 | tf_op jit(solution)/shard_map/ppermute | solution.py:20
  72.4 15.1 %collective-permute-start.9 = (f32[128,4,128]{2,0,1:T(8,128)S(1)}, f32[128,4,128]{2,0,1:T(8,128)S(1)}, u32[]{:S(2)}, u32[]{:S(2)}) collective-permute-start(f32[128,4,128]{2,0,1:T(8,128)S(1)} %fusion.50), channel_id=1, source_target_pairs={{0,1},{1,2},{2,3},{3,4},{4,5},{5,6},{6,7},{7,8},{8,9},{9,10},{10,1... | collective-permute-start | bytes 786440 | tf_op jit(solution)/shard_map/ppermute | solution.py:20
  77.1 13.9 %collective-permute-start.14 = (f32[128,4,128]{2,0,1:T(8,128)S(1)}, f32[128,4,128]{2,0,1:T(8,128)S(1)}, u32[]{:S(2)}, u32[]{:S(2)}) collective-permute-start(f32[128,4,128]{2,0,1:T(8,128)S(1)} %fusion.51), channel_id=1, source_target_pairs={{0,1},{1,2},{2,3},{3,4},{4,5},{5,6},{6,7},{7,8},{8,9},{9,10},{10,1... | collective-permute-start | bytes 786440 | tf_op jit(solution)/shard_map/ppermute | solution.py:20
  87.5 13.7 %collective-permute-start.10 = (f32[128,4,128]{2,0,1:T(8,128)S(1)}, f32[128,4,128]{2,0,1:T(8,128)S(1)}, u32[]{:S(2)}, u32[]{:S(2)}) collective-permute-start(f32[128,4,128]{2,0,1:T(8,128)S(1)} %add.235), channel_id=1, source_target_pairs={{0,1},{1,2},{2,3},{3,4},{4,5},{5,6},{6,7},{7,8},{8,9},{9,10},{10,1... | collective-permute-start | bytes 786440 | tf_op jit(solution)/shard_map/ppermute | solution.py:20
  91.1 13.1 %copy-start.6 = (f32[128,4,128]{2,0,1:T(8,128)S(1)}, f32[128,4,128]{2,0,1:T(8,128)}, u32[]{:S(2)}) copy-start(f32[128,4,128]{2,0,1:T(8,128)} %convolution_bitcast_fusion.1) | copy-start | bytes 786436
  91.1 13.1 %collective-permute-start.15 = (f32[128,4,128]{2,0,1:T(8,128)S(1)}, f32[128,4,128]{2,0,1:T(8,128)S(1)}, u32[]{:S(2)}, u32[]{:S(2)}) collective-permute-start(f32[128,4,128]{2,0,1:T(8,128)S(1)} %add.239), channel_id=1, source_target_pairs={{0,1},{1,2},{2,3},{3,4},{4,5},{5,6},{6,7},{7,8},{8,9},{9,10},{10,1... | collective-permute-start | bytes 786440 | tf_op jit(solution)/shard_map/ppermute | solution.py:20
  101.3 14.1 %collective-permute-start.11 = (f32[128,4,128]{2,0,1:T(8,128)S(1)}, f32[128,4,128]{2,0,1:T(8,128)S(1)}, u32[]{:S(2)}, u32[]{:S(2)}) collective-permute-start(f32[128,4,128]{2,0,1:T(8,128)S(1)} %add.236), channel_id=1, source_target_pairs={{0,1},{1,2},{2,3},{3,4},{4,5},{5,6},{6,7},{7,8},{8,9},{9,10},{10,1... | collective-permute-start | bytes 786440 | tf_op jit(solution)/shard_map/ppermute | solution.py:20
  104.2 13.2 %copy-start.8 = (f32[128,4,128]{2,0,1:T(8,128)S(1)}, f32[128,4,128]{2,0,1:T(8,128)}, u32[]{:S(2)}) copy-start(f32[128,4,128]{2,0,1:T(8,128)} %convolution_bitcast_fusion) | copy-start | bytes 786436
  104.2 15.1 %copy-start.5 = (bf16[128,4,128]{2,0,1:T(8,128)(2,1)S(1)}, bf16[128,4,128]{2,0,1:T(8,128)(2,1)}, u32[]{:S(2)}) copy-start(bf16[128,4,128]{2,0,1:T(8,128)(2,1)} %copy-done.4) | copy-start | bytes 393220
  104.2 13.1 %collective-permute-start.16 = (f32[128,4,128]{2,0,1:T(8,128)S(1)}, f32[128,4,128]{2,0,1:T(8,128)S(1)}, u32[]{:S(2)}, u32[]{:S(2)}) collective-permute-start(f32[128,4,128]{2,0,1:T(8,128)S(1)} %add.240), channel_id=1, source_target_pairs={{0,1},{1,2},{2,3},{3,4},{4,5},{5,6},{6,7},{7,8},{8,9},{9,10},{10,1... | collective-permute-start | bytes 786440 | tf_op jit(solution)/shard_map/ppermute | solution.py:20
  115.4 20.5 %collective-permute-start.12 = (bf16[128,4,128]{2,0,1:T(8,128)(2,1)S(1)}, bf16[128,4,128]{2,0,1:T(8,128)(2,1)S(1)}, u32[]{:S(2)}, u32[]{:S(2)}) collective-permute-start(bf16[128,4,128]{2,0,1:T(8,128)(2,1)S(1)} %add_convert_fusion.2), channel_id=1, source_target_pairs={{0,508},{1,509},{2,510},{3,511},{4,0},{5,1},{6,2},{7,3},{8,4},{9,5... | collective-permute-start | bytes 393224 | tf_op jit(solution)/shard_map/ppermute | solution.py:20
  117.4 23.2 %collective-permute-start.17 = (bf16[128,4,128]{2,0,1:T(8,128)(2,1)S(1)}, bf16[128,4,128]{2,0,1:T(8,128)(2,1)S(1)}, u32[]{:S(2)}, u32[]{:S(2)}) collective-permute-start(bf16[128,4,128]{2,0,1:T(8,128)(2,1)S(1)} %add_convert_fusion.1), channel_id=1, source_target_pairs={{0,508},{1,509},{2,510},{3,511},{4,0},{5,1},{6,2},{7,3},{8,4},{9,5... | collective-permute-start | bytes 393224 | tf_op jit(solution)/shard_map/ppermute | solution.py:20
  (4 other events, 8.1 us)
where the time goes:
time: 142 us; the launch traced here: 141 us
  starting transfers between devices  89.1 us (63%)
  matrix products  22.9 us (16%)
  waiting for transfers between devices  18.1 us (13%)
  local copies, waits for them, and re-layouts  6.25 us (4%)
  other arithmetic  3.76 us (3%)
    ppermute x10, starting transfers between devices, shifted(): lax.ppermute(shard, axis, [(i, (i + by) % peers) for i in range(peers)])  55.2 us
    ppermute x8, starting transfers between devices, from_behind(): return lax.ppermute(shard, axis, pairs)  34 us
    ppermute x10, waiting for transfers between devices, shifted(): lax.ppermute(shard, axis, [(i, (i + by) % peers) for i in range(peers)])  18 us
    dot_general x5, matrix products, partial_value(): jnp.einsum('kgts,tkgd->skd', weights, grad_four, preferred_element_type=j...  7.25 us
    unnamed x25, local copies, waits for them, and re-layouts  5.45 us
    dot_general x5, matrix products, project(): jnp.einsum('tkgd,skd->kgts', grad_four, value_block, preferred_element_ty...  5.03 us
    dot_general x5, matrix products, project(): jnp.einsum('tkgd,skd->kgts', query_four, key_block, preferred_element_typ...  4.65 us
    convert_element_type x1, other arithmetic, partial_value(): (score_scale * prob * (grad_weights - row_delta[..., None])).astype(jnp.b...  3.32 us
  transfers between devices with their start and end apart: 18, of which 3 were waited for; matrix products, arithmetic and copies ran while one was open for 13% of the time, Pallas kernels for 0%

commit v1 on v0

v1 whole, which is shorter than its diff:
```python
import jax
import jax.numpy as jnp
from jax import lax
from jax.experimental import pallas as pl
from jax.experimental.pallas import tpu as pltpu
from jax.sharding import PartitionSpec as P

QH = 32
KVH = 4
HD = 128
SPAN = 4
GROUP = QH // KVH
MESH = pl.DeviceIdType.MESH
SCALE = HD**-0.5
SCALE2 = SCALE * 1.4426950408889634
HIDDEN = -1e30
F32 = jnp.float32
BF16 = jnp.bfloat16


def dot(a, b, dim_a, dim_b):
    return lax.dot_general(a, b, (((dim_a,), (dim_b,)), ((), ())), preferred_element_type=F32)


def make_kernel(devices, inner, rows, chunk):
    halo = SPAN * rows
    span = halo + rows
    band = halo + chunk

    def kernel(
        q_hbm, k_ref, v_ref, g_hbm, b_ref,
        dq_ref, dk_ref, dv_ref,
        q_in, g_in, q16, g16, kv, hide, acc, wide, dq32,
        to_near, to_other, near_in, other_in, far_out, far_in, own_out, own_in,
        in_sem, kv_send, kv_recv, pair_send, pair_recv, back_send, back_recv,
    ):
        me = lax.axis_index("outer") * inner + lax.axis_index("inner")
        odd = lax.rem(me, 2)
        even = odd == 0
        partner = me + 1 - 2 * odd

        def at(index):
            return (index // inner, lax.rem(index, inner))

        q_copy = pltpu.make_async_copy(q_hbm, q_in, in_sem.at[0])
        g_copy = pltpu.make_async_copy(g_hbm, g_in, in_sem.at[1])
        q_copy.start()
        g_copy.start()

        has_before = me >= 2
        has_after = me + 2 < devices

        for part, ref in ((0, k_ref), (1, v_ref)):
            wide[part] = ref[...].astype(F32)
            for c in range(KVH):
                own = wide[part, pl.ds(c, rows, stride=KVH), :]
                kv[c, part, pl.ds(halo, rows), :] = own.astype(BF16)

        @pl.when(me < SPAN)
        def _():
            kv[:, :, pl.ds(0, halo), :] = jnp.zeros((KVH, 2, halo, HD), BF16)

        @pl.when(jnp.logical_not(has_after))
        def _():
            far_in[...] = jnp.zeros(far_in.shape, BF16)
            own_in[...] = jnp.zeros(own_in.shape, BF16)

        barrier = pltpu.get_barrier_semaphore()

        @pl.when(has_before)
        def _():
            pl.semaphore_signal(barrier, inc=1, device_id=at(me - 2), device_id_type=MESH)

        @pl.when(odd == 1)
        def _():
            pl.semaphore_signal(barrier, inc=1, device_id=at(partner), device_id_type=MESH)

        waits = (1 - odd) + has_after.astype(jnp.int32)

        @pl.when(waits > 0)
        def _():
            pl.semaphore_wait(barrier, waits)

        def block(c, offset):
            start = (SPAN - offset) * rows
            if not isinstance(start, int):
                start = pl.multiple_of(start, rows)
            return kv.at[c, :, pl.ds(start, rows), :]

        def ahead(c, offset):
            kind = offset // 2
            return pltpu.make_async_remote_copy(
                block(c, offset), block(c, offset + 2), kv_send.at[kind, c], kv_recv.at[kind, c],
                device_id=at(me + 2), device_id_type=MESH,
            )

        def across(c, offset):
            kind = 2 + offset // 2
            return pltpu.make_async_remote_copy(
                block(c, offset - 1 + 2 * odd), block(c, offset), kv_send.at[kind, c],
                kv_recv.at[kind, c], device_id=at(partner), device_id_type=MESH,
            )

        def own_ahead(c):
            @pl.when(has_after)
            def _():
                ahead(c, 0).start()

        def relay(c):
            @pl.when(odd == 1)
            def _():
                across(c, 1).wait_recv()

            @pl.when(has_before)
            def _():
                ahead(c, 0).wait_recv()

                @pl.when(has_after)
                def _():
                    ahead(c, 2).start()

                @pl.when(even)
                def _():
                    across(c, 3).start()

                @pl.when(odd == 1)
                def _():
                    across(c, 1).start()

        def relay_last(c):
            @pl.when(me >= 4)
            def _():
                ahead(c, 2).wait_recv()

                @pl.when(odd == 1)
                def _():
                    across(c, 3).start()

        def all_here(c):
            @pl.when(even & has_before)
            def _():
                across(c, 1).wait_recv()

            @pl.when((me >= 4) | (me == 3))
            def _():
                across(c, 3).wait_recv()

        own_ahead(0)
        own_ahead(1)

        @pl.when(even)
        def _():
            for c in range(KVH):
                across(c, 1).start()

        base = (me - SPAN) * rows
        pos = lax.broadcasted_iota(jnp.int32, (span, rows), 0) + base
        query = lax.broadcasted_iota(jnp.int32, (span, rows), 1) + (base + halo)
        seen = (
            (pos >= b_ref[0:1, :])
            & (pos <= query)
            & ((pos < b_ref[1:2, :]) | (pos >= b_ref[2:3, :]))
        )
        hide[...] = jnp.where(seen, 0.0, HIDDEN).astype(BF16)

        def arrange(copy, source, target):
            copy.wait()
            for half in range(QH // 16):
                x = source[:, pl.ds(16 * half, 16), :].astype(F32)
                for k in range(16 // GROUP):
                    y = x[:, GROUP * k : GROUP * (k + 1), :].reshape(rows * GROUP, HD)
                    target[half * (16 // GROUP) + k] = y.astype(BF16)

        arrange(q_copy, q_in, q16)
        arrange(g_copy, g_in, g16)

        def compute(c, j):
            many = chunk * GROUP
            first = j * chunk
            key = kv[c, 0, pl.ds(first, band), :]
            value = kv[c, 1, pl.ds(first, band), :]
            queries = q16[c, pl.ds(first * GROUP, many), :]
            grads = g16[c, pl.ds(first * GROUP, many), :]
            lane = lax.broadcasted_iota(jnp.int32, (many, rows), 1)
            token = lax.broadcasted_iota(jnp.int32, (many, rows), 0) // GROUP + first
            mine = (lane == token).astype(BF16)
            scores = dot(
                jnp.concatenate([key, hide[pl.ds(first, band), :]], axis=1),
                jnp.concatenate([queries, mine], axis=1),
                1, 1,
            )
            grad_weights = dot(value, grads, 1, 1)
            top = jnp.max(scores, axis=0, keepdims=True)
            raw = jnp.exp2(scores * SCALE2 - top * SCALE2)
            total = jnp.sum(raw, axis=0, keepdims=True)
            weighted = jnp.sum(raw * grad_weights, axis=0, keepdims=True)
            inverse = 1.0 / total
            prob = raw * inverse
            dscore = (prob * (grad_weights - weighted * inverse)).astype(BF16)
            weights = prob.astype(BF16)
            for part, left, right in ((0, dscore, queries), (1, weights, grads)):
                add = dot(left, right, 1, 0)
                if j == 0:
                    acc[c, part, pl.ds(0, band), :] = add
                    acc[c, part, pl.ds(band, span - band), :] = jnp.zeros((span - band, HD), F32)
                else:
                    acc[c, part, pl.ds(first, band), :] += add
            query_part = dot(dscore, key, 0, 0) * SCALE
            dq32[pl.ds(first, chunk), pl.ds(GROUP * c, GROUP), :] = query_part.reshape(
                chunk, GROUP, HD
            )

        def pair(c, kind, source, target):
            return pltpu.make_async_remote_copy(
                source.at[c], target.at[c], pair_send.at[kind, c], pair_recv.at[kind, c],
                device_id=at(partner), device_id_type=MESH,
            )

        def back(c, kind, source, target):
            return pltpu.make_async_remote_copy(
                source.at[c], target.at[c], back_send.at[kind, c], back_recv.at[kind, c],
                device_id=at(me - 2), device_id_type=MESH,
            )

        odd_f = odd.astype(F32)

        def send_pair(c):
            near = pl.multiple_of(halo - rows - 2 * rows * odd, rows)
            other = pl.multiple_of(rows + 2 * rows * odd, rows)
            to_other[c] = acc[c, :, pl.ds(other, rows), :].astype(BF16)
            pair(c, 0, to_other, other_in).start()
            to_near[c] = acc[c, :, pl.ds(near, rows), :].astype(BF16)
            pair(c, 1, to_near, near_in).start()

        def send_far(c):
            pair(c, 0, to_other, other_in).wait_recv()
            far = acc[c, :, pl.ds(0, rows), :] + odd_f * other_in[c].astype(F32)
            far_out[c] = far.astype(BF16)

            @pl.when(has_before)
            def _():
                back(c, 0, far_out, far_in).start()

        def send_own(c):
            pair(c, 1, to_near, near_in).wait_recv()

            @pl.when(has_after)
            def _():
                back(c, 0, far_out, far_in).wait_recv()

            near = acc[c, :, pl.ds(2 * rows, rows), :] + near_in[c].astype(F32)
            own_out[c] = (near + far_in[c].astype(F32)).astype(BF16)

            @pl.when(has_before)
            def _():
                back(c, 1, own_out, own_in).start()

        def finish(c):
            @pl.when(has_after)
            def _():
                back(c, 1, own_out, own_in).wait_recv()

            own = acc[c, :, pl.ds(halo, rows), :] + (1.0 - odd_f) * other_in[c].astype(F32)
            own = own + own_in[c].astype(F32)
            wide[0, pl.ds(c, rows, stride=KVH), :] = own[0] * SCALE
            wide[1, pl.ds(c, rows, stride=KVH), :] = own[1]

        relay(0)
        own_ahead(2)
        relay_last(0)
        relay(1)
        own_ahead(3)
        for c in range(KVH):
            if c + 2 < KVH:
                relay(c + 2)
            if c + 1 < KVH:
                relay_last(c + 1)
            all_here(c)
            for j in range(rows // chunk):
                compute(c, j)
            send_pair(c)
            if c >= 1:
                send_far(c - 1)
            if c >= 2:
                send_own(c - 2)
            if c % 2 == 1:
                pick = pl.ds(GROUP * (c - 1), 2 * GROUP)
                dq_ref[:, pick, :] = dq32[:, pick, :].astype(BF16)
        send_far(KVH - 1)
        send_own(KVH - 2)
        finish(0)
        finish(1)
        send_own(KVH - 1)
        finish(2)
        finish(3)
        dk_ref[...] = wide[0].astype(BF16)
        dv_ref[...] = wide[1].astype(BF16)

        for c in range(KVH):
            pair(c, 0, to_other, other_in).wait_send()
            pair(c, 1, to_near, near_in).wait_send()

            @pl.when(has_before)
            def _():
                back(c, 0, far_out, far_in).wait_send()
                back(c, 1, own_out, own_in).wait_send()

            @pl.when(has_after)
            def _():
                ahead(c, 0).wait_send()

                @pl.when(has_before)
                def _():
                    ahead(c, 2).wait_send()

            @pl.when(even | has_before)
            def _():
                across(c, 1).wait_send()

            @pl.when((even & has_before) | (me >= 4))
            def _():
                across(c, 3).wait_send()

    return kernel


def solution(mesh):
    outer, inner = mesh.shape["outer"], mesh.shape["inner"]
    devices = outer * inner

    def per_device(queries, key_states, value_states, out_grad, bounds):
        rows = queries.shape[0]
        chunk = min(64, rows // 2)
        span = (SPAN + 1) * rows
        piece = pltpu.VMEM((KVH, 2, rows, HD), BF16)
        vmem = pl.BlockSpec(memory_space=pltpu.VMEM)
        anywhere = pl.BlockSpec(memory_space=pl.ANY)
        flat = (rows * KVH, HD)
        query_grad, key_grad, value_grad = pl.pallas_call(
            make_kernel(devices, inner, rows, chunk),
            out_shape=[
                jax.ShapeDtypeStruct((rows, QH, HD), BF16),
                jax.ShapeDtypeStruct(flat, BF16),
                jax.ShapeDtypeStruct(flat, BF16),
            ],
            in_specs=[anywhere, vmem, vmem, anywhere, vmem],
            out_specs=[vmem, vmem, vmem],
            scratch_shapes=[
                pltpu.VMEM((rows, QH, HD), BF16),
                pltpu.VMEM((rows, QH, HD), BF16),
                pltpu.VMEM((KVH, rows * GROUP, HD), BF16),
                pltpu.VMEM((KVH, rows * GROUP, HD), BF16),
                pltpu.VMEM((KVH, 2, span, HD), BF16),
                pltpu.VMEM((span, rows), BF16),
                pltpu.VMEM((KVH, 2, span, HD), F32),
                pltpu.VMEM((2, rows * KVH, HD), F32),
                pltpu.VMEM((rows, QH, HD), F32),
                piece, piece, piece, piece, piece, piece, piece, piece,
                pltpu.SemaphoreType.DMA((2,)),
                pltpu.SemaphoreType.DMA((4, KVH)),
                pltpu.SemaphoreType.DMA((4, KVH)),
                pltpu.SemaphoreType.DMA((2, KVH)),
                pltpu.SemaphoreType.DMA((2, KVH)),
                pltpu.SemaphoreType.DMA((2, KVH)),
                pltpu.SemaphoreType.DMA((2, KVH)),
            ],
            compiler_params=pltpu.CompilerParams(
                collective_id=0, has_side_effects=True, vmem_limit_bytes=48 * 2**20
            ),
            cost_estimate=pl.CostEstimate(
                flops=10 * QH * rows * span * HD,
                bytes_accessed=8 * rows * (QH + KVH) * HD,
                transcendentals=QH * rows * span,
            ),
        )(
            queries, key_states.reshape(flat), value_states.reshape(flat), out_grad, bounds
        )
        back = key_states.shape
        return query_grad, key_grad.reshape(back), value_grad.reshape(back)

    split = ("outer", "inner")
    whole = P(split, None, None)
    return jax.shard_map(
        per_device,
        mesh=mesh,
        in_specs=(whole, whole, whole, whole, P(None, split)),
        out_specs=(whole, whole, whole),
        check_vma=False,
    )
```

time: 142 us -> 53.2 us (0.37)
  the two profiles are of different devices: /device:TPU:252 before, /device:TPU:254 now
where the time goes in v1:
time: 53.2 us; the launch traced here: 53 us
  Pallas kernels  45.1 us (85%)
  local copies, waits for them, and re-layouts  7.21 us (14%)
  between operations  0.65 us (1%)
    pallas_call x1, Pallas kernels, per_device(): pl.pallas_call(make_kernel(devices, inner, rows, chunk), out_shape=[jax.S...  45.1 us
    unnamed x13, local copies, waits for them, and re-layouts  7.21 us

profile of v1, /device:TPU:254, one launch (start us, length us, event | category | flops | bytes accessed | tf_op | source)
XLA Modules:
  0.0 53.0 jit_solution(17033045389736761502)
XLA Ops:
  0.6 0.0 copy-start.4
  0.6 0.7 %copy-done.4 = s32[3,128]{1,0:T(4,128)S(1)} copy-done((s32[3,128]{1,0:T(4,128)S(1)}, s32[3,128]{1,0:T(4,128)}, u32[]{:S(2)}) %copy-start.4) | copy-done | bytes 1560
  1.3 0.0 copy-start
  1.3 1.2 %copy-done = bf16[128,32,128]{2,1,0:T(8,128)(2,1)S(1)} copy-done((bf16[128,32,128]{2,1,0:T(8,128)(2,1)S(1)}, bf16[128,32,128]{2,1,0:T(8,128)(2,1)}, u32[]{:S(2)}) %copy-start) | copy-done | bytes 1048600
  2.5 0.0 copy-start.1
  2.5 1.2 %copy-done.1 = bf16[128,32,128]{2,1,0:T(8,128)(2,1)S(1)} copy-done((bf16[128,32,128]{2,1,0:T(8,128)(2,1)S(1)}, bf16[128,32,128]{2,1,0:T(8,128)(2,1)}, u32[]{:S(2)}) %copy-start.1) | copy-done | bytes 1048600
  3.8 0.0 copy-start.2
  3.8 0.9 %copy-done.2 = bf16[128,4,128]{2,1,0:T(4,128)(2,1)S(1)} copy-done((bf16[128,4,128]{2,1,0:T(4,128)(2,1)S(1)}, bf16[128,4,128]{2,1,0:T(4,128)(2,1)}, u32[]{:S(2)}) %copy-start.2) | copy-done | bytes 131096
  4.7 0.0 copy-start.3
  4.7 0.9 %copy-done.3 = bf16[128,4,128]{2,1,0:T(4,128)(2,1)S(1)} copy-done((bf16[128,4,128]{2,1,0:T(4,128)(2,1)S(1)}, bf16[128,4,128]{2,1,0:T(4,128)(2,1)}, u32[]{:S(2)}) %copy-start.3) | copy-done | bytes 131096
  5.6 45.1 %shard_map.76 = (bf16[128,32,128]{2,1,0:T(8,128)(2,1)S(1)}, bf16[512,128]{1,0:T(8,128)(2,1)S(1)}, bf16[512,128]{1,0:T(8,128)(2,1)S(1)}) custom-call(bf16[128,32,128]{2,1,0:T(8,128)(2,1)S(1)} %copy-done, bf16[512,128]{1,0:T(8,128)(2,1)S(1)} %bitcast.6, bf16[512,128]{1,0:T(8,128)(2,1)S(1)} %bitcast.7, bf16[128,32,128]{2,1,0:T(8,128)(2,1)S(1)} %copy-done.1, ...), custom_call_target="tpu_custom_call" | custom-call | flops 3355443200 | bytes 4718592 | tf_op jit(solution)/shard_map/pallas_call | solution.py:339
  50.7 1.0 %copy.11 = bf16[128,32,128]{2,1,0:T(8,128)(2,1)} copy(bf16[128,32,128]{2,1,0:T(8,128)(2,1)S(1)} %get-tuple-element.12) | data formatting | bytes 2097152
  51.7 0.7 %copy.12 = bf16[128,4,128]{2,1,0:T(4,128)(2,1)} copy(bf16[128,4,128]{2,1,0:T(4,128)(2,1)S(1)} %bitcast.5) | data formatting | bytes 262144
  52.3 0.7 %copy.13 = bf16[128,4,128]{2,1,0:T(4,128)(2,1)} copy(bf16[128,4,128]{2,1,0:T(4,128)(2,1)S(1)} %bitcast.4) | data formatting | bytes 262144
Async XLA Ops:
  0.6 0.7 %copy-start.4 = (s32[3,128]{1,0:T(4,128)S(1)}, s32[3,128]{1,0:T(4,128)}, u32[]{:S(2)}) copy-start(s32[3,128]{1,0:T(4,128)} %b_ref.1) | copy-start | bytes 4612
  1.3 1.2 %copy-start = (bf16[128,32,128]{2,1,0:T(8,128)(2,1)S(1)}, bf16[128,32,128]{2,1,0:T(8,128)(2,1)}, u32[]{:S(2)}) copy-start(bf16[128,32,128]{2,1,0:T(8,128)(2,1)} %q_hbm.1) | copy-start | bytes 3145732
  2.5 1.2 %copy-start.1 = (bf16[128,32,128]{2,1,0:T(8,128)(2,1)S(1)}, bf16[128,32,128]{2,1,0:T(8,128)(2,1)}, u32[]{:S(2)}) copy-start(bf16[128,32,128]{2,1,0:T(8,128)(2,1)} %g_hbm.1) | copy-start | bytes 3145732
  3.8 0.9 %copy-start.2 = (bf16[128,4,128]{2,1,0:T(4,128)(2,1)S(1)}, bf16[128,4,128]{2,1,0:T(4,128)(2,1)}, u32[]{:S(2)}) copy-start(bf16[128,4,128]{2,1,0:T(4,128)(2,1)} %param.6) | copy-start | bytes 393220
  4.7 0.9 %copy-start.3 = (bf16[128,4,128]{2,1,0:T(4,128)(2,1)S(1)}, bf16[128,4,128]{2,1,0:T(4,128)(2,1)}, u32[]{:S(2)}) copy-start(bf16[128,4,128]{2,1,0:T(4,128)(2,1)} %param.7) | copy-start | bytes 393220

commit v2 on v1

--- a/solution.py
+++ b/solution.py
@@ -28,11 +28,11 @@
     band = halo + chunk
 
     def kernel(
-        q_hbm, k_ref, v_ref, g_hbm, b_ref,
-        dq_ref, dk_ref, dv_ref,
-        q_in, g_in, q16, g16, kv, hide, acc, wide, dq32,
+        q_hbm, k_hbm, v_hbm, g_hbm, b_hbm,
+        dq_hbm, dk_hbm, dv_hbm,
+        q_in, g_in, k_in, v_in, b_in, dq_out, q16, g16, kv, hide, acc, wide, dq32,
         to_near, to_other, near_in, other_in, far_out, far_in, own_out, own_in,
-        in_sem, kv_send, kv_recv, pair_send, pair_recv, back_send, back_recv,
+        in_sem, out_sem, kv_send, kv_recv, pair_send, pair_recv, back_send, back_recv,
     ):
         me = lax.axis_index("outer") * inner + lax.axis_index("inner")
         odd = lax.rem(me, 2)
@@ -42,40 +42,41 @@
         def at(index):
             return (index // inner, lax.rem(index, inner))
 
-        q_copy = pltpu.make_async_copy(q_hbm, q_in, in_sem.at[0])
-        g_copy = pltpu.make_async_copy(g_hbm, g_in, in_sem.at[1])
-        q_copy.start()
-        g_copy.start()
-
         has_before = me >= 2
         has_after = me + 2 < devices
-
-        for part, ref in ((0, k_ref), (1, v_ref)):
+        far_before = me >= SPAN
+        far_after = me + SPAN < devices
+
+        barrier = pltpu.get_barrier_semaphore()
+        for step, there in ((2, has_before), (SPAN, far_before)):
+
+            @pl.when(there)
+            def _():
+                pl.semaphore_signal(
+                    barrier, inc=1, device_id=at(me - step), device_id_type=MESH
+                )
+
+        @pl.when(odd == 1)
+        def _():
+            pl.semaphore_signal(barrier, inc=1, device_id=at(partner), device_id_type=MESH)
+
+        copies = [
+            pltpu.make_async_copy(source, target, in_sem.at[i])
+            for i, (source, target) in enumerate(
+                ((k_hbm, k_in), (v_hbm, v_in), (b_hbm, b_in), (q_hbm, q_in), (g_hbm, g_in))
+            )
+        ]
+        for copy in copies:
+            copy.start()
+
+        for part, ref in ((0, k_in), (1, v_in)):
+            copies[part].wait()
             wide[part] = ref[...].astype(F32)
             for c in range(KVH):
                 own = wide[part, pl.ds(c, rows, stride=KVH), :]
                 kv[c, part, pl.ds(halo, rows), :] = own.astype(BF16)
 
-        @pl.when(me < SPAN)
-        def _():
-            kv[:, :, pl.ds(0, halo), :] = jnp.zeros((KVH, 2, halo, HD), BF16)
-
-        @pl.when(jnp.logical_not(has_after))
-        def _():
-            far_in[...] = jnp.zeros(far_in.shape, BF16)
-            own_in[...] = jnp.zeros(own_in.shape, BF16)
-
-        barrier = pltpu.get_barrier_semaphore()
-
-        @pl.when(has_before)
-        def _():
-            pl.semaphore_signal(barrier, inc=1, device_id=at(me - 2), device_id_type=MESH)
-
-        @pl.when(odd == 1)
-        def _():
-            pl.semaphore_signal(barrier, inc=1, device_id=at(partner), device_id_type=MESH)
-
-        waits = (1 - odd) + has_after.astype(jnp.int32)
+        waits = (1 - odd) + has_after.astype(jnp.int32) + far_after.astype(jnp.int32)
 
         @pl.when(waits > 0)
         def _():
@@ -88,10 +89,9 @@
             return kv.at[c, :, pl.ds(start, rows), :]
 
         def ahead(c, offset):
-            kind = offset // 2
             return pltpu.make_async_remote_copy(
-                block(c, offset), block(c, offset + 2), kv_send.at[kind, c], kv_recv.at[kind, c],
-                device_id=at(me + 2), device_id_type=MESH,
+                block(c, 0), block(c, offset), kv_send.at[offset // 2 - 1, c],
+                kv_recv.at[offset // 2 - 1, c], device_id=at(me + offset), device_id_type=MESH,
             )
 
         def across(c, offset):
@@ -104,7 +104,22 @@
         def own_ahead(c):
             @pl.when(has_after)
             def _():
-                ahead(c, 0).start()
+                ahead(c, 2).start()
+
+            @pl.when(far_after)
+            def _():
+                ahead(c, SPAN).start()
+
+        def next_ahead(c):
+            @pl.when(has_after)
+            def _():
+                ahead(c - 1, 2).wait_send()
+
+            @pl.when(far_after)
+            def _():
+                ahead(c - 1, SPAN).wait_send()
+
+            own_ahead(c)
 
         def relay(c):
             @pl.when(odd == 1)
@@ -113,11 +128,7 @@
 
             @pl.when(has_before)
             def _():
-                ahead(c, 0).wait_recv()
-
-                @pl.when(has_after)
-                def _():
-                    ahead(c, 2).start()
+                ahead(c, 2).wait_recv()
 
                 @pl.when(even)
                 def _():
@@ -127,10 +138,10 @@
                 def _():
                     across(c, 1).start()
 
-        def relay_last(c):
-            @pl.when(me >= 4)
-            def _():
-                ahead(c, 2).wait_recv()
+        def relay_far(c):
+            @pl.when(far_before)
+            def _():
+                ahead(c, SPAN).wait_recv()
 
                 @pl.when(odd == 1)
                 def _():
@@ -141,18 +152,36 @@
             def _():
                 across(c, 1).wait_recv()
 
-            @pl.when((me >= 4) | (me == 3))
+            @pl.when(far_before | (me == 3))
             def _():
                 across(c, 3).wait_recv()
 
         own_ahead(0)
-        own_ahead(1)
 
         @pl.when(even)
         def _():
             for c in range(KVH):
                 across(c, 1).start()
 
+        for offset in range(1, SPAN + 1):
+
+            @pl.when(me < offset)
+            def _():
+                for c in range(KVH):
+                    kv[c, :, pl.ds((SPAN - offset) * rows, rows), :] = jnp.zeros(
+                        (2, rows, HD), BF16
+                    )
+
+        @pl.when(jnp.logical_not(has_after))
+        def _():
+            own_in[...] = jnp.zeros(own_in.shape, BF16)
+
+        @pl.when(jnp.logical_not(far_after))
+        def _():
+            far_in[...] = jnp.zeros(far_in.shape, BF16)
+
+        copies[2].wait()
+        b_ref = b_in
         base = (me - SPAN) * rows
         pos = lax.broadcasted_iota(jnp.int32, (span, rows), 0) + base
         query = lax.broadcasted_iota(jnp.int32, (span, rows), 1) + (base + halo)
@@ -171,8 +200,9 @@
                     y = x[:, GROUP * k : GROUP * (k + 1), :].reshape(rows * GROUP, HD)
                     target[half * (16 // GROUP) + k] = y.astype(BF16)
 
-        arrange(q_copy, q_in, q16)
-        arrange(g_copy, g_in, g16)
+        arrange(copies[3], q_in, q16)
+        next_ahead(1)
+        arrange(copies[4], g_in, g16)
 
         def compute(c, j):
             many = chunk * GROUP
@@ -219,7 +249,7 @@
         def back(c, kind, source, target):
             return pltpu.make_async_remote_copy(
                 source.at[c], target.at[c], back_send.at[kind, c], back_recv.at[kind, c],
-                device_id=at(me - 2), device_id_type=MESH,
+                device_id=at(me - 2 - 2 * kind), device_id_type=MESH,
             )
 
         odd_f = odd.astype(F32)
@@ -232,69 +262,77 @@
             to_near[c] = acc[c, :, pl.ds(near, rows), :].astype(BF16)
             pair(c, 1, to_near, near_in).start()
 
-        def send_far(c):
+        def send_back(c):
             pair(c, 0, to_other, other_in).wait_recv()
             far = acc[c, :, pl.ds(0, rows), :] + odd_f * other_in[c].astype(F32)
             far_out[c] = far.astype(BF16)
 
+            @pl.when(far_before)
+            def _():
+                back(c, 1, far_out, far_in).start()
+
+            pair(c, 1, to_near, near_in).wait_recv()
+            near = acc[c, :, pl.ds(2 * rows, rows), :] + near_in[c].astype(F32)
+            own_out[c] = near.astype(BF16)
+
             @pl.when(has_before)
             def _():
-                back(c, 0, far_out, far_in).start()
-
-        def send_own(c):
-            pair(c, 1, to_near, near_in).wait_recv()
+                back(c, 0, own_out, own_in).start()
+
+        def finish(c):
+            own = acc[c, :, pl.ds(halo, rows), :] + (1.0 - odd_f) * other_in[c].astype(F32)
 
             @pl.when(has_after)
             def _():
-                back(c, 0, far_out, far_in).wait_recv()
-
-            near = acc[c, :, pl.ds(2 * rows, rows), :] + near_in[c].astype(F32)
-            own_out[c] = (near + far_in[c].astype(F32)).astype(BF16)
-
-            @pl.when(has_before)
-            def _():
-                back(c, 1, own_out, own_in).start()
-
-        def finish(c):
-            @pl.when(has_after)
-            def _():
-                back(c, 1, own_out, own_in).wait_recv()
-
-            own = acc[c, :, pl.ds(halo, rows), :] + (1.0 - odd_f) * other_in[c].astype(F32)
-            own = own + own_in[c].astype(F32)
+                back(c, 0, own_out, own_in).wait_recv()
+
+            @pl.when(far_after)
+            def _():
+                back(c, 1, far_out, far_in).wait_recv()
+
+            own = own + own_in[c].astype(F32) + far_in[c].astype(F32)
             wide[0, pl.ds(c, rows, stride=KVH), :] = own[0] * SCALE
             wide[1, pl.ds(c, rows, stride=KVH), :] = own[1]
 
         relay(0)
-        own_ahead(2)
-        relay_last(0)
-        relay(1)
-        own_ahead(3)
+        relay_far(0)
+        next_ahead(2)
+        all_here(0)
         for c in range(KVH):
-            if c + 2 < KVH:
-                relay(c + 2)
-            if c + 1 < KVH:
-                relay_last(c + 1)
-            all_here(c)
+            if c > 0:
+                all_here(c)
             for j in range(rows // chunk):
                 compute(c, j)
+                if j == 0:
+                    if c == 0:
+                        next_ahead(3)
+                    if c + 1 < KVH:
+                        relay(c + 1)
+                    if c >= 1:
+                        send_back(c - 1)
+                    if c + 1 < KVH:
+                        relay_far(c + 1)
             send_pair(c)
-            if c >= 1:
-                send_far(c - 1)
-            if c >= 2:
-                send_own(c - 2)
             if c % 2 == 1:
                 pick = pl.ds(GROUP * (c - 1), 2 * GROUP)
-                dq_ref[:, pick, :] = dq32[:, pick, :].astype(BF16)
-        send_far(KVH - 1)
-        send_own(KVH - 2)
+                dq_out[:, pick, :] = dq32[:, pick, :].astype(BF16)
+                copy = pltpu.make_async_copy(
+                    dq_out.at[:, pick, :], dq_hbm.at[:, pick, :], out_sem.at[c // 2]
+                )
+                copy.start()
+                copies.append(copy)
         finish(0)
+        send_back(KVH - 1)
         finish(1)
-        send_own(KVH - 1)
         finish(2)
         finish(3)
-        dk_ref[...] = wide[0].astype(BF16)
-        dv_ref[...] = wide[1].astype(BF16)
+        for part, (source, target) in enumerate(((k_in, dk_hbm), (v_in, dv_hbm))):
+            source[...] = wide[part].astype(BF16)
+            copy = pltpu.make_async_copy(source, target, out_sem.at[2 + part])
+            copy.start()
+            copies.append(copy)
+        for copy in copies[5:]:
+            copy.wait()
 
         for c in range(KVH):
             pair(c, 0, to_other, other_in).wait_send()
@@ -302,26 +340,55 @@
 
             @pl.when(has_before)
             def _():
-                back(c, 0, far_out, far_in).wait_send()
-                back(c, 1, own_out, own_in).wait_send()
-
-            @pl.when(has_after)
-            def _():
-                ahead(c, 0).wait_send()
-
-                @pl.when(has_before)
+                back(c, 0, own_out, own_in).wait_send()
+
+            @pl.when(far_before)
+            def _():
+                back(c, 1, far_out, far_in).wait_send()
+
+            if c == KVH - 1:
+
+                @pl.when(has_after)
                 def _():
                     ahead(c, 2).wait_send()
 
+                @pl.when(far_after)
+                def _():
+                    ahead(c, SPAN).wait_send()
+
             @pl.when(even | has_before)
             def _():
                 across(c, 1).wait_send()
 
-            @pl.when((even & has_before) | (me >= 4))
+            @pl.when((even & has_before) | far_before)
             def _():
                 across(c, 3).wait_send()
 
     return kernel
+
+
+def write_out(*refs):
+    sources, targets, spaces, (sems,) = refs[:3], refs[3:6], refs[6:9], refs[9:]
+    pieces = []
+    for source, target, space in zip(sources, targets, spaces):
+        cuts = 4 if len(source.shape) == 3 else 1
+        size = source.shape[0] // cuts
+        for i in range(cuts):
+            pick = pl.ds(i * size, size)
+            n = len(pieces)
+            pieces.append(
+                (
+                    pltpu.make_async_copy(source.at[pick], space.at[pick], sems.at[0, n]),
+                    pltpu.make_async_copy(space.at[pick], target.at[pick], sems.at[1, n]),
+                )
+            )
+    for inward, _ in pieces:
+        inward.start()
+    for inward, outward in pieces:
+        inward.wait()
+        outward.start()
+    for _, outward in pieces:
+        outward.wait()
 
 
 def solution(mesh):
@@ -333,8 +400,7 @@
         chunk = min(64, rows // 2)
         span = (SPAN + 1) * rows
         piece = pltpu.VMEM((KVH, 2, rows, HD), BF16)
-        vmem = pl.BlockSpec(memory_space=pltpu.VMEM)
-        anywhere = pl.BlockSpec(memory_space=pl.ANY)
+        hbm = pl.BlockSpec(memory_space=pltpu.HBM)
         flat = (rows * KVH, HD)
         query_grad, key_grad, value_grad = pl.pallas_call(
             make_kernel(devices, inner, rows, chunk),
@@ -343,10 +409,14 @@
                 jax.ShapeDtypeStruct(flat, BF16),
                 jax.ShapeDtypeStruct(flat, BF16),
             ],
-            in_specs=[anywhere, vmem, vmem, anywhere, vmem],
-            out_specs=[vmem, vmem, vmem],
+            in_specs=[hbm] * 5,
+            out_specs=[hbm] * 3,
             scratch_shapes=[
                 pltpu.VMEM((rows, QH, HD), BF16),
+                pltpu.VMEM((rows, QH, HD), BF16),
+                pltpu.VMEM(flat, BF16),
+                pltpu.VMEM(flat, BF16),
+                pltpu.VMEM(bounds.shape, jnp.int32),
                 pltpu.VMEM((rows, QH, HD), BF16),
                 pltpu.VMEM((KVH, rows * GROUP, HD), BF16),
                 pltpu.VMEM((KVH, rows * GROUP, HD), BF16),
@@ -356,7 +426,8 @@
                 pltpu.VMEM((2, rows * KVH, HD), F32),
                 pltpu.VMEM((rows, QH, HD), F32),
                 piece, piece, piece, piece, piece, piece, piece, piece,
-                pltpu.SemaphoreType.DMA((2,)),
+                pltpu.SemaphoreType.DMA((5,)),
+                pltpu.SemaphoreType.DMA((4,)),
                 pltpu.SemaphoreType.DMA((4, KVH)),
                 pltpu.SemaphoreType.DMA((4, KVH)),
                 pltpu.SemaphoreType.DMA((2, KVH)),
@@ -365,7 +436,7 @@
                 pltpu.SemaphoreType.DMA((2, KVH)),
             ],
             compiler_params=pltpu.CompilerParams(
-                collective_id=0, has_side_effects=True, vmem_limit_bytes=48 * 2**20
+                collective_id=0, has_side_effects=True, vmem_limit_bytes=56 * 2**20
             ),
             cost_estimate=pl.CostEstimate(
                 flops=10 * QH * rows * span * HD,
@@ -375,6 +446,16 @@
         )(
             queries, key_states.reshape(flat), value_states.reshape(flat), out_grad, bounds
         )
+        grads = (query_grad, key_grad, value_grad)
+        query_grad, key_grad, value_grad = pl.pallas_call(
+            write_out,
+            out_shape=[jax.ShapeDtypeStruct(x.shape, x.dtype) for x in grads],
+            in_specs=[hbm] * 3,
+            out_specs=[hbm] * 3,
+            scratch_shapes=[pltpu.VMEM(x.shape, x.dtype) for x in grads]
+            + [pltpu.SemaphoreType.DMA((2, 6))],
+            compiler_params=pltpu.CompilerParams(vmem_limit_bytes=56 * 2**20),
+        )(*grads)
         back = key_states.shape
         return query_grad, key_grad.reshape(back), value_grad.reshape(back)
 

time: 53.2 us -> 43.7 us (0.82)
  the two profiles are of different devices: /device:TPU:254 before, /device:TPU:37 now
where the time goes in v2:
time: 43.7 us; the launch traced here: 43.5 us
  Pallas kernels  42.9 us (98%)
  between operations  0.64 us (1%)
    pallas_call x1, Pallas kernels, per_device(): pl.pallas_call(make_kernel(devices, inner, rows, chunk), out_shape=[jax.S...  40.8 us
    pallas_call x1, Pallas kernels, per_device(): pl.pallas_call(write_out, out_shape=[jax.ShapeDtypeStruct(x.shape, x.dtyp...  2.1 us

profile of v2, /device:TPU:37, one launch (start us, length us, event | category | flops | bytes accessed | tf_op | source)
XLA Modules:
  0.0 43.5 jit_solution(3487129086543703280)
XLA Ops:
  0.6 40.8 %shard_map.76 = (bf16[128,32,128]{2,1,0:T(8,128)(2,1)}, bf16[512,128]{1,0:T(8,128)(2,1)}, bf16[512,128]{1,0:T(8,128)(2,1)}) custom-call(bf16[128,32,128]{2,1,0:T(8,128)(2,1)} %q_hbm.1, bf16[512,128]{1,0:T(8,128)(2,1)} %bitcast.4, bf16[512,128]{1,0:T(8,128)(2,1)} %bitcast.5, bf16[128,32,128]{2,1,0:T(8,128)(2,1)} %g_hbm.1, s32[3,128]{1,0:T(4,128)} %b_hbm.1), custom_call_target="tpu_custom_call" | custom-call | flops 3355443200 | bytes 4718592 | tf_op jit(solution)/shard_map/pallas_call | solution.py:405
  41.4 2.1 %shard_map.77 = (bf16[128,32,128]{2,1,0:T(8,128)(2,1)}, bf16[512,128]{1,0:T(8,128)(2,1)}, bf16[512,128]{1,0:T(8,128)(2,1)}) custom-call(bf16[128,32,128]{2,1,0:T(8,128)(2,1)} %get-tuple-element.9.refs_0_, bf16[512,128]{1,0:T(8,128)(2,1)} %get-tuple-element.10.refs_1_, bf16[512,128]{1,0:T(8,128)(2,1)} %get-tuple-element.11.refs_2_), custom_call_target="tpu_custom_call" | custom-call | tf_op jit(solution)/shard_map/pallas_call | solution.py:450

commit v3 on v2

--- a/solution.py
+++ b/solution.py
@@ -257,12 +257,20 @@
         def send_pair(c):
             near = pl.multiple_of(halo - rows - 2 * rows * odd, rows)
             other = pl.multiple_of(rows + 2 * rows * odd, rows)
+            to_near[c] = acc[c, :, pl.ds(near, rows), :].astype(BF16)
+            pair(c, 1, to_near, near_in).start()
             to_other[c] = acc[c, :, pl.ds(other, rows), :].astype(BF16)
             pair(c, 0, to_other, other_in).start()
-            to_near[c] = acc[c, :, pl.ds(near, rows), :].astype(BF16)
-            pair(c, 1, to_near, near_in).start()
 
         def send_back(c):
+            pair(c, 1, to_near, near_in).wait_recv()
+            near = acc[c, :, pl.ds(2 * rows, rows), :] + near_in[c].astype(F32)
+            own_out[c] = near.astype(BF16)
+
+            @pl.when(has_before)
+            def _():
+                back(c, 0, own_out, own_in).start()
+
             pair(c, 0, to_other, other_in).wait_recv()
             far = acc[c, :, pl.ds(0, rows), :] + odd_f * other_in[c].astype(F32)
             far_out[c] = far.astype(BF16)
@@ -271,14 +279,6 @@
             def _():
                 back(c, 1, far_out, far_in).start()
 
-            pair(c, 1, to_near, near_in).wait_recv()
-            near = acc[c, :, pl.ds(2 * rows, rows), :] + near_in[c].astype(F32)
-            own_out[c] = near.astype(BF16)
-
-            @pl.when(has_before)
-            def _():
-                back(c, 0, own_out, own_in).start()
-
         def finish(c):
             own = acc[c, :, pl.ds(halo, rows), :] + (1.0 - odd_f) * other_in[c].astype(F32)
 
@@ -294,25 +294,20 @@
             wide[0, pl.ds(c, rows, stride=KVH), :] = own[0] * SCALE
             wide[1, pl.ds(c, rows, stride=KVH), :] = own[1]
 
+        next_ahead(2)
         relay(0)
         relay_far(0)
-        next_ahead(2)
-        all_here(0)
+        next_ahead(3)
         for c in range(KVH):
-            if c > 0:
-                all_here(c)
+            all_here(c)
+            if c >= 1:
+                send_back(c - 1)
             for j in range(rows // chunk):
                 compute(c, j)
-                if j == 0:
-                    if c == 0:
-                        next_ahead(3)
-                    if c + 1 < KVH:
-                        relay(c + 1)
-                    if c >= 1:
-                        send_back(c - 1)
-                    if c + 1 < KVH:
-                        relay_far(c + 1)
             send_pair(c)
+            if c + 1 < KVH:
+                relay(c + 1)
+                relay_far(c + 1)
             if c % 2 == 1:
                 pick = pl.ds(GROUP * (c - 1), 2 * GROUP)
                 dq_out[:, pick, :] = dq32[:, pick, :].astype(BF16)

time: 43.7 us -> 43.3 us (level)
  the two profiles are of different devices: /device:TPU:37 before, /device:TPU:252 now
where the time goes in v3:
time: 43.3 us; the launch traced here: 43.1 us
  Pallas kernels  42.5 us (98%)
  between operations  0.64 us (1%)
    pallas_call x1, Pallas kernels, per_device(): pl.pallas_call(make_kernel(devices, inner, rows, chunk), out_shape=[jax.S...  40.4 us
    pallas_call x1, Pallas kernels, per_device(): pl.pallas_call(write_out, out_shape=[jax.ShapeDtypeStruct(x.shape, x.dtyp...  2.1 us

profile of v3, /device:TPU:252, one launch (start us, length us, event | category | flops | bytes accessed | tf_op | source)
XLA Modules:
  0.0 43.1 jit_solution(2036686933221920531)
XLA Ops:
  0.6 40.4 %shard_map.76 = (bf16[128,32,128]{2,1,0:T(8,128)(2,1)}, bf16[512,128]{1,0:T(8,128)(2,1)}, bf16[512,128]{1,0:T(8,128)(2,1)}) custom-call(bf16[128,32,128]{2,1,0:T(8,128)(2,1)} %q_hbm.1, bf16[512,128]{1,0:T(8,128)(2,1)} %bitcast.4, bf16[512,128]{1,0:T(8,128)(2,1)} %bitcast.5, bf16[128,32,128]{2,1,0:T(8,128)(2,1)} %g_hbm.1, s32[3,128]{1,0:T(4,128)} %b_hbm.1), custom_call_target="tpu_custom_call" | custom-call | flops 3355443200 | bytes 4718592 | tf_op jit(solution)/shard_map/pallas_call | solution.py:400
  41.0 2.1 %shard_map.77 = (bf16[128,32,128]{2,1,0:T(8,128)(2,1)}, bf16[512,128]{1,0:T(8,128)(2,1)}, bf16[512,128]{1,0:T(8,128)(2,1)}) custom-call(bf16[128,32,128]{2,1,0:T(8,128)(2,1)} %get-tuple-element.9.refs_0_, bf16[512,128]{1,0:T(8,128)(2,1)} %get-tuple-element.10.refs_1_, bf16[512,128]{1,0:T(8,128)(2,1)} %get-tuple-element.11.refs_2_), custom_call_target="tpu_custom_call" | custom-call | tf_op jit(solution)/shard_map/pallas_call | solution.py:445
